TPU v7x, 128 devices: a whole 4x4x4 slice. The times are simulated.
128 devices in a mesh: gx: 4 (over x), gy: 32 (over y, z, core).
Axes of the slice: x: 4, y: 4, z: 4, core: 2. Of those that a mesh axis runs over, the one named last changes fastest.
Arguments:
- multipole: bfloat16 [32768, 256], P(('gx', 'gy')), may hold values from -6 to 6
- coarse_multipole: bfloat16 [4096, 256], P(('gx', 'gy')), may hold values from -6 to 6
- operators: bfloat16 [48, 256, 256], replicated, may hold values from -0.0390625 to 0.0390625
- source_list: int32 [32768, 189], P(('gx', 'gy')), may hold values from 0 to 32767, as said below
- op_list: int32 [32768, 189], P(('gx', 'gy')), may hold values from 0 to 47
- list_count: int32 [32768], P(('gx', 'gy')), may hold values from 1 to 189, as said below
- coarse_src: int32 [32768, 27], P(('gx', 'gy')), may hold values from 0 to 4095
- coarse_op: int32 [32768, 27], P(('gx', 'gy')), may hold values from 0 to 47
Outputs:
- local_expansion: float32 [32768, 256], P(('gx', 'gy'))
Inputs may be any that keep to these rules, and one draw needn't show every extreme that they name: source_list[t, j] is a block of owner(t) - 1, owner(t) or owner(t) + 1 (owner(b) = b // 256). `list_count`: the first block of every device uses all 189 slots.
All inputs are finite; a program needn't handle non-finite values.
Results may differ from a plain program's by a relative error of at most 0.0055.
Values may be sent and summed in bfloat16 or wider, within the bound.
A program may use at most 128 MiB of HBM per device.

v0:
```python
import jax
import jax.numpy as jnp
from jax import lax
from jax.sharding import PartitionSpec as P


def with_halo(shard, sides, width):
    for axis, dim in sides:
        size, length = (lax.axis_size(axis), shard.shape[dim])
        up = [(i, (i + 1) % size) for i in range(size - 1)]
        down = [(j, i) for i, j in up]
        last = lax.slice_in_dim(shard, length - width, length, axis=dim)
        first = lax.slice_in_dim(shard, 0, width, axis=dim)
        before = lax.ppermute(last, axis, up)
        after = lax.ppermute(first, axis, down)
        shard = jnp.concatenate([before, shard, after], axis=dim)
    return shard


def tally_slots(ops, located, valid, nops, width):
    op_hot = ((ops[:, :, None] == jnp.arange(nops, dtype=jnp.int32)) & valid[:, :, None]).astype(
        jnp.bfloat16
    )
    src_hot = (located[:, :, None] == jnp.arange(width, dtype=jnp.int32)).astype(jnp.bfloat16)
    return jnp.einsum("tjr,tjc->trc", op_hot, src_hot, preferred_element_type=jnp.float32).astype(
        jnp.bfloat16
    )


def translate(tally, window, operators, sides):
    blocks, nops, width = tally.shape
    per_side = width // sides
    coeffs = window.shape[1]
    group = jnp.einsum(
        "trsc,scp->tsrp",
        tally.reshape(blocks, nops, sides, per_side),
        window.reshape(sides, per_side, coeffs),
        preferred_element_type=jnp.float32,
    ).astype(jnp.bfloat16)
    return jnp.einsum("tsrp,rqp->tq", group, operators, preferred_element_type=jnp.float32)


def local(
    multipole, coarse_multipole, operators, source_list, op_list, list_count, coarse_src, coarse_op
):
    blocks = multipole.shape[0]
    slots = source_list.shape[1]
    nops = operators.shape[0]
    me = lax.axis_index(("gx", "gy"))
    gathered = lax.all_gather(coarse_multipole, ("gx", "gy"), axis=0, tiled=True)
    valid = jnp.arange(slots, dtype=jnp.int32)[None, :] < list_count[:, None]
    located = source_list - (me - 1) * blocks
    window = with_halo(multipole, ((("gx", "gy"), 0),), blocks)
    tally = tally_slots(op_list, located, valid, nops, 3 * blocks)
    near = translate(tally, window, operators, 3)
    picked = gathered[coarse_src]
    cop_hot = (coarse_op[:, :, None] == jnp.arange(nops, dtype=jnp.int32)).astype(jnp.bfloat16)
    coarse_group = jnp.einsum(
        "tjr,tjp->trp", cop_hot, picked, preferred_element_type=jnp.float32
    ).astype(jnp.bfloat16)
    far = jnp.einsum("trp,rqp->tq", coarse_group, operators, preferred_element_type=jnp.float32)
    return near + far


def solution(mesh):
    placed = (
        P(("gx", "gy"), None),
        P(("gx", "gy"), None),
        P(),
        P(("gx", "gy"), None),
        P(("gx", "gy"), None),
        P(("gx", "gy")),
        P(("gx", "gy"), None),
        P(("gx", "gy"), None),
    )
    return jax.shard_map(
        local, mesh=mesh, in_specs=placed, out_specs=P(("gx", "gy"), None), check_vma=False
    )
```

profile of v0, /device:TPU:6, one launch (start us, length us, event | category | flops | bytes accessed | tf_op | source)
XLA Modules:
  0.0 155.1 jit_solution(11354434867317478673)
XLA Ops:
  6.5 0.0 all-gather.2.cloned.1.call-start
  6.5 1.9 %collective-permute-start = (bf16[256,256]{1,0:T(8,128)(2,1)}, bf16[256,256]{1,0:T(8,128)(2,1)}, u32[]{:S(2)}, u32[]{:S(2)}) collective-permute-start(bf16[256,256]{1,0:T(8,128)(2,1)} %param.8), channel_id=1, source_target_pairs={{0,1},{1,2},{2,3},{3,4},{4,5},{5,6},{6,7},{7,8},{8,9},{9,10},{10,1... | collective-permute-start | bytes 393224 | tf_op jit(solution)/shard_map/ppermute | solution.py:14
  8.5 8.1 %collective-permute-start.1 = (bf16[256,256]{1,0:T(8,128)(2,1)}, bf16[256,256]{1,0:T(8,128)(2,1)}, u32[]{:S(2)}, u32[]{:S(2)}) collective-permute-start(bf16[256,256]{1,0:T(8,128)(2,1)} %param.8), channel_id=1, source_target_pairs={{1,0},{2,1},{3,2},{4,3},{5,4},{6,5},{7,6},{8,7},{9,8},{10,9},{11,1... | collective-permute-start | bytes 393224 | tf_op jit(solution)/shard_map/ppermute | solution.py:15
  16.6 0.0 all-gather.2.cloned.1.call-update
  16.6 1.1 copy.26
  17.7 0.8 iota_compare_fusion.9
  18.5 3.2 %fusion.31 = pred[256,189,48]{1,2,0:T(8,128)(4,1)S(1)} fusion(s32[256,189]{1,0:T(8,128)S(1)} %copy.26, pred[256,189]{1,0:T(8,128)(4,1)S(1)} %iota_compare_fusion.9), kind=kLoop, calls=%fused_computation.10.clone.clone.clone.clone.2 | loop fusion | flops 4644864 | bytes 2564352 | tf_op jit(solution)/shard_map/tjr,tjc->trc/dot_general | solution.py:25
  21.7 0.9 broadcast_subtract_fusion
  22.6 0.8 copy.27
  23.5 35.7 %fusion.7 = bf16[256,48,768]{2,1,0:T(8,128)(2,1)} fusion(s32[256,189]{1,0:T(8,128)} %copy.27, pred[256,189,48]{1,2,0:T(8,128)(4,1)S(1)} %fusion.31), kind=kOutput, calls=%fused_computation.11 | convolution fusion | flops 3613851648 | bytes 21390336 | tf_op jit(solution)/shard_map/tjr,tjc->trc/dot_general | solution.py:25
  59.2 0.0 copy-done.2
  59.2 0.0 copy-start.1
  59.2 24.5 %copy.28 = bf16[256,48,768]{0,2,1:T(8,128)(2,1)} copy(bf16[256,48,768]{2,1,0:T(8,128)(2,1)} %fusion.7) | data formatting | bytes 37748736 | tf_op jit(solution)/shard_map/convert_element_type | solution.py:25
  83.7 0.1 copy.34
  83.8 0.2 reshape.34
  84.0 0.0 copy-done.1
  84.0 0.8 copy.33
  84.8 9.1 %copy.32 = bf16[48,256,256]{1,0,2:T(8,128)(2,1)} copy(bf16[48,256,256]{2,1,0:T(8,128)(2,1)} %param.10) | data formatting | bytes 12582912 | tf_op args[2]
  93.9 0.6 pad_clamp_fusion
  94.5 0.0 collective-permute-done
  94.6 0.0 collective-permute-done.1
  94.6 0.0 copy-done
  94.6 1.0 pad_maximum_fusion
  95.6 13.4 %convert_reduce_fusion = bf16[256,256,48]{1,0,2:T(8,128)(2,1)} fusion(bf16[3,256,256,1]{2,1,3,0:T(8,128)(2,1)S(1)} %bitcast.27, bf16[256,48,3,256]{0,3,2,1:T(8,128)(2,1)} %bitcast.24), kind=kOutput, calls=%fused_computation.4 | convolution fusion | flops 4857004032 | bytes 25559040 | tf_op jit(solution)/shard_map/trsc,scp->tsrp/dot_general | solution.py:34
  109.0 18.4 %gather_fusion = bf16[6912,256]{1,0:T(8,128)(2,1)S(1)} fusion(bf16[4096,256]{1,0:T(8,128)(2,1)} %all-gather.2.cloned.1.call-done, s32[7168]{0:T(1024)} %pad_clamp_fusion), kind=kCustom, calls=%fused_computation | custom fusion | bytes 7105536 | tf_op jit(solution)/shard_map/gather | solution.py:56
  127.4 2.9 %reshape.33 = bf16[256,27,256]{2,1,0:T(8,128)(2,1)} reshape(bf16[6912,256]{1,0:T(8,128)(2,1)S(1)} %gather_fusion) | data formatting | bytes 7077888 | tf_op jit(solution)/shard_map/gather | solution.py:56
  130.3 5.6 %fusion.17 = bf16[256,48,256]{2,1,0:T(8,128)(2,1)S(1)} fusion(bf16[256,27,256]{2,1,0:T(8,128)(2,1)} %reshape.33, s32[256,27]{1,0:T(8,128)} %copy.33), kind=kOutput, calls=%fused_computation.18 | convolution fusion | flops 173346816 | bytes 9858048 | tf_op jit(solution)/shard_map/tjr,tjp->trp/dot_general | solution.py:58
  135.9 0.0 slice-start.1
  135.9 0.0 slice-start.3
  135.9 6.7 %fusion.19 = f32[256,256]{1,0:T(8,128)S(1)} fusion(bf16[48,256,256]{2,1,0:T(8,128)(2,1)} %param.10, bf16[256,48,256]{2,1,0:T(8,128)(2,1)S(1)} %fusion.17), kind=kOutput, calls=%fused_computation.20 | convolution fusion | flops 1610612736 | bytes 12845056 | tf_op jit(solution)/shard_map/trp,rqp->tq/dot_general | solution.py:61
  142.6 0.0 slice-done
  142.7 5.6 %fusion.23 = f32[256,256]{1,0:T(8,128)} fusion(f32[256,256]{1,0:T(8,128)S(1)} %fusion.19, bf16[48,256,256]{1,0,2:T(8,128)(2,1)S(1)} %bitcast.26, bf16[256,256,48]{1,0,2:T(8,128)(2,1)S(1)} %bitcast.29), kind=kOutput, calls=%fused_computation.22 | convolution fusion | flops 1610678272 | bytes 13107200 | tf_op jit(solution)/shard_map/tsrp,rqp->tq/dot_general | solution.py:40
  (11 shorter events, 0.0 us)
Async XLA Ops:
  6.5 102.4 %all-gather.2.cloned.1.call-start = ((), (), s32[]{:S(2)}) async-start(), calls=%async_computation | async-start | bytes 2113536 | tf_op jit(solution)/shard_map/all_gather | solution.py:50
  6.5 88.0 %collective-permute-start = (bf16[256,256]{1,0:T(8,128)(2,1)}, bf16[256,256]{1,0:T(8,128)(2,1)}, u32[]{:S(2)}, u32[]{:S(2)}) collective-permute-start(bf16[256,256]{1,0:T(8,128)(2,1)} %param.8), channel_id=1, source_target_pairs={{0,1},{1,2},{2,3},{3,4},{4,5},{5,6},{6,7},{7,8},{8,9},{9,10},{10,1... | collective-permute-start | bytes 393224 | tf_op jit(solution)/shard_map/ppermute | solution.py:14
  8.5 86.1 %collective-permute-start.1 = (bf16[256,256]{1,0:T(8,128)(2,1)}, bf16[256,256]{1,0:T(8,128)(2,1)}, u32[]{:S(2)}, u32[]{:S(2)}) collective-permute-start(bf16[256,256]{1,0:T(8,128)(2,1)} %param.8), channel_id=1, source_target_pairs={{1,0},{2,1},{3,2},{4,3},{5,4},{6,5},{7,6},{8,7},{9,8},{10,9},{11,1... | collective-permute-start | bytes 393224 | tf_op jit(solution)/shard_map/ppermute | solution.py:15
  23.5 35.7 %copy-start.2 = (s32[256,27]{0,1:T(8,128)S(1)}, s32[256,27]{0,1:T(8,128)}, u32[]{:S(2)}) copy-start(s32[256,27]{0,1:T(8,128)} %param.14) | copy-start | bytes 82948
  59.2 24.8 %copy-start.1 = (s32[256,27]{0,1:T(8,128)S(1)}, s32[256,27]{0,1:T(8,128)}, u32[]{:S(2)}) copy-start(s32[256,27]{0,1:T(8,128)} %param.15) | copy-start | bytes 82948
  84.8 9.7 %copy-start = (bf16[256,256]{1,0:T(8,128)(2,1)S(1)}, bf16[256,256]{1,0:T(8,128)(2,1)}, u32[]{:S(2)}) copy-start(bf16[256,256]{1,0:T(8,128)(2,1)} %param.8) | copy-start | bytes 393220
  130.3 12.4 %slice-start = ((s8[6291456]{0:T(1024)(128)(4,1)}), s8[4194304]{0:T(1024)(128)(4,1)S(1)}, s32[]{:S(2)}) async-start(s8[6291456]{0:T(1024)(128)(4,1)} %bitcast.25), calls=%async_computation.1 | async-start | bytes 8388608
  130.3 12.4 %slice-start.2 = ((s8[6291456]{0:T(1024)(128)(4,1)}), s8[4194304]{0:T(1024)(128)(4,1)S(1)}, s32[]{:S(2)}) async-start(s8[6291456]{0:T(1024)(128)(4,1)} %bitcast.28), calls=%async_computation.3 | async-start | bytes 8388608
  135.9 6.8 %slice-start.1 = ((s8[6291456]{0:T(1024)(128)(4,1)}), s8[2097152]{0:T(1024)(128)(4,1)S(1)}, s32[]{:S(2)}) async-start(s8[6291456]{0:T(1024)(128)(4,1)} %bitcast.25), calls=%async_computation.2 | async-start | bytes 4194304
  135.9 6.8 %slice-start.3 = ((s8[6291456]{0:T(1024)(128)(4,1)}), s8[2097152]{0:T(1024)(128)(4,1)S(1)}, s32[]{:S(2)}) async-start(s8[6291456]{0:T(1024)(128)(4,1)} %bitcast.28), calls=%async_computation.4 | async-start | bytes 4194304
Sparse Core Ops, SparseCore 0:
  16.7 61.3 all-gather.1
where the time goes:
time: 157 us; the launch traced here: 155 us
  matrix products  67 us (43%)
  local copies, waits for them, and re-layouts  57.9 us (37%)
  between operations  13.6 us (9%)
  starting transfers between devices  10 us (6%)
  other arithmetic  6.55 us (4%)
    dot_general x1, matrix products, tally_slots(): jnp.einsum('tjr,tjc->trc', op_hot, src_hot, preferred_element_type=jnp.fl...  35.7 us
    convert_element_type x1, local copies, waits for them, and re-layouts, tally_slots(): jnp.einsum('tjr,tjc->trc', op_hot, src_hot, preferred_element_type=jnp.fl...  24.5 us
    gather x2, local copies, waits for them, and re-layouts, local(): picked = gathered[coarse_src]  21.3 us
    dot_general x1, matrix products, translate(): jnp.einsum('trsc,scp->tsrp', tally.reshape(blocks, nops, sides, per_side)...  13.4 us
    unnamed x17, local copies, waits for them, and re-layouts  11 us
    ppermute x1, starting transfers between devices, with_halo(): after = lax.ppermute(first, axis, down)  8.1 us
    dot_general x1, matrix products, local(): jnp.einsum('trp,rqp->tq', coarse_group, operators, preferred_element_type...  6.72 us
    dot_general x1, matrix products, local(): jnp.einsum('tjr,tjp->trp', cop_hot, picked, preferred_element_type=jnp.fl...  5.6 us
  transfers between devices with their start and end apart: 3, of which 0 were waited for; matrix products, arithmetic and copies ran while one was open for 60% of the time, Pallas kernels for 0%

commit v1 on v0

v1 whole, which is shorter than its diff:
```python
import functools

import jax
import jax.numpy as jnp
from jax import lax
from jax.experimental import pallas as pl
from jax.experimental.pallas import tpu as pltpu
from jax.sharding import PartitionSpec as P

TARGETS = 256
SLOTS = 189
COARSE_SLOTS = 27
NOPS = 48
COEFFS = 256
STEP = 16
F8 = jnp.float8_e4m3fn
BF16 = jnp.bfloat16
F32 = jnp.float32
LAST = (((1,), (1,)), ((), ()))
MESH = pl.DeviceIdType.MESH

ORDERS = ((2, 1, 0), (0, 2, 1), (1, 0, 2), (2, 1, 0))


def one_hot_rows(row, blocks):
    number = lax.broadcasted_iota(jnp.int32, row.shape, 0).astype(F32)
    one, zero = BF16(1), BF16(0)
    return jnp.concatenate(
        [jnp.where(row == (number + 16.0 * k).astype(BF16), one, zero) for k in range(blocks)], axis=0
    )


def transpose8(v):
    row = lax.broadcasted_iota(jnp.int32, v[0].shape, 0)
    cur = [v[0]] + [pltpu.roll(v[k], k, 0) for k in range(1, 8)]
    for bit in (1, 2, 4):
        odd = (row & bit) != 0
        cur = [jnp.where(odd, cur[(k + bit) % 8], cur[k]) for k in range(8)]
    return [cur[0]] + [pltpu.roll(cur[8 - r], 8 - r, 0) for r in range(1, 8)]


def kernel(
    multipole, coarse, operators, source_t, op_t, count, coarse_src_t, coarse_op_t,
    out,
    window, received, table, ops, src_v, op_v, count_v, cop_v, csrc, slot_q, slot_c, slot_cop, tmp, tally, picked0, picked1, group,
    local_sem, send_sem, recv_sem, sib_send, sib_recv, halo_send, halo_recv,
):
    x = lax.axis_index("gx")
    gy = lax.axis_index("gy")
    y, z, core = lax.div(gy, 8), lax.rem(lax.div(gy, 2), 4), lax.rem(gy, 2)
    coords = (x, y, z)
    me = x * 32 + gy

    def device(cx, cy, cz, cc):
        return (cx, (cy * 4 + cz) * 2 + cc)

    def linear(d):
        return (lax.div(d, 32), lax.rem(d, 32))

    def local(src, dst, k):
        return pltpu.make_async_copy(src, dst, local_sem.at[k])

    rows16 = lambda f, pos, n: received.at[f, pl.ds(pl.multiple_of(pos * 16, 16), n * 16), :]
    flow = [core * 2 + h for h in range(2)]
    at = []
    for h in range(2):
        at.append([coords[ORDERS[h][s]] * (1 - core) + coords[ORDERS[2 + h][s]] * core for s in range(3)])

    def region(h, stage, last=None):
        a, b, c = at[h]
        c = c if last is None else last
        if stage == 0:
            return rows16(flow[h], c * 16 + b * 4 + a, 1)
        if stage == 1:
            return rows16(flow[h], c * 16 + b * 4, 4)
        return rows16(flow[h], c * 16, 16)

    own = [local(coarse.at[pl.ds(h * 16, 16), :], region(h, 0), h) for h in range(2)]
    mid = local(multipole, window.at[pl.ds(256, 256), :], 2)
    lists = [
        local(source_t, src_v, 3), local(op_t, op_v, 4), local(count, count_v, 5), local(coarse_op_t, cop_v, 6),
        local(coarse_src_t, csrc, 7),
    ]
    weights = local(operators, ops, 8)
    for c in own + [mid] + lists + [weights]:
        c.start()

    barrier = pltpu.get_barrier_semaphore()
    after, before = linear(lax.rem(me + 1, 128)), linear(lax.rem(me + 127, 128))
    partners = [device(x, y, z, 1 - core), after, before]
    for axis in range(3):
        for k in range(1, 4):
            other = list(coords)
            other[axis] = lax.rem(coords[axis] + k, 4)
            partners.append(device(*other, core))
    for p in partners:
        pl.semaphore_signal(barrier, inc=1, device_id=p, device_id_type=MESH)

    def hop(h, stage, k):
        other = list(coords)
        for c, weight in ((0, 1 - core), (1, core)):
            axis = ORDERS[2 * c + h][stage]
            other[axis] = other[axis] + weight * (lax.rem(coords[axis] + k, 4) - coords[axis])
        part = region(h, stage)
        return pltpu.make_async_remote_copy(
            src_ref=part, dst_ref=part, send_sem=send_sem.at[h, stage, k - 1], recv_sem=recv_sem.at[h, stage, k - 1],
            device_id=device(*other, core), device_id_type=MESH,
        )

    def to_sibling(h, k):
        part = region(h, 2, lax.rem(at[h][2] + 4 - k, 4))
        return pltpu.make_async_remote_copy(
            src_ref=part, dst_ref=part, send_sem=sib_send.at[h, k], recv_sem=sib_recv.at[h, k],
            device_id=device(x, y, z, 1 - core), device_id_type=MESH,
        )

    def halo(k):
        return pltpu.make_async_remote_copy(
            src_ref=window.at[pl.ds(256, 256), :], dst_ref=window.at[pl.ds(512 * k, 256), :],
            send_sem=halo_send.at[k], recv_sem=halo_recv.at[k], device_id=(after, before)[k], device_id_type=MESH,
        )

    hops = [(h, k) for k in (1, 3, 2) for h in range(2)]

    for c in lists[:3]:
        c.wait()
    place = src_v[...] - (me - 1) * TARGETS
    slot = lax.broadcasted_iota(jnp.int32, (SLOTS, TARGETS), 0)
    joint = jnp.where(slot < count_v[...], lax.shift_right_arithmetic(place, 8) * NOPS + op_v[...], -1)
    tmp[...] = jnp.full((256, 256), -1.0, F32)
    tmp[:SLOTS, :] = joint.astype(F32)
    slot_q[...] = tmp[...].T
    tmp[:SLOTS, :] = (place & 255).astype(F32)
    slot_c[...] = tmp[...].T

    for c in own + [mid]:
        c.wait()
    pl.semaphore_wait(barrier, len(partners))
    for h, k in hops:
        hop(h, 0, k).start()
    halo(0).start()
    halo(1).start()

    for c in lists[3:]:
        c.wait()
    tmp[:128, :] = jnp.full((128, 256), -1.0, F32)
    tmp[:COARSE_SLOTS, :] = cop_v[...].astype(F32)
    slot_cop[...] = tmp[:128, :].T
    picked0[...] = jnp.zeros_like(picked0)
    picked1[...] = jnp.zeros_like(picked1)

    def count_slots(i, _):
        @pl.when(i == 3)
        def _():
            for h, k in hops:
                hop(h, 0, k).wait_recv()
            for h, k in hops:
                hop(h, 1, k).start()

        @pl.when(i == 8)
        def _():
            for h, k in hops:
                hop(h, 1, k).wait_recv()
            for h, k in hops:
                hop(h, 2, k).start()
            for h in range(2):
                to_sibling(h, 0).start()

        for u in range(STEP):
            t = i * STEP + u
            q = jnp.broadcast_to(slot_q[pl.ds(t, 1), :], (16, 256)).astype(BF16)
            c = jnp.broadcast_to(slot_c[pl.ds(t, 1), :], (16, 256)).astype(BF16)
            hot_q = one_hot_rows(q, 9).astype(F8)
            hot_c = one_hot_rows(c, 16).astype(F8)
            n = lax.dot_general(hot_q, hot_c, LAST, preferred_element_type=F32).astype(BF16)
            for s in range(3):
                tally[s, pl.ds(pl.multiple_of(t * NOPS, NOPS), NOPS), :] = n[s * NOPS : (s + 1) * NOPS]
        return 0

    lax.fori_loop(0, TARGETS // STEP, count_slots, 0)

    for k in (1, 3, 2):
        for h in range(2):
            hop(h, 2, k).wait_recv()
            to_sibling(h, k).start()
    for k in range(2):
        halo(k).wait_recv()
    for k in (0, 1, 3, 2):
        for h in range(2):
            to_sibling(h, k).wait_recv()

    def fill(i, _):
        cx, cy, cz = lax.div(i, 16), lax.rem(lax.div(i, 4), 4), lax.rem(i, 4)
        chip = (cx, cy, cz)
        for f in range(4):
            a, b, c = (chip[ORDERS[f][s]] for s in range(3))
            v = received[f, pl.ds(pl.multiple_of((c * 16 + b * 4 + a) * 16, 16), 16), :].astype(F32)
            row = pl.ds(pl.multiple_of(i * 64 + f * 16, 16), 16)
            table[row, 0, :] = v[:, :128]
            table[row, 1, :] = v[:, 128:]
        return 0

    lax.fori_loop(0, 64, fill, 0)

    number = lax.broadcasted_iota(jnp.int32, (NOPS, 32), 0).astype(F32)

    def gather(t0, picked):
        for u in range(STEP):
            for j in range(COARSE_SLOTS):
                picked[pl.ds((u * 32 + j) * 2, 2), :] = table[csrc[j, t0 + u]]

    def groups(t0, picked):
        rows = pl.ds(pl.multiple_of(t0 * NOPS, STEP * NOPS), STEP * NOPS)
        near = jnp.zeros((STEP * NOPS, COEFFS), F32)
        for s in range(3):
            near = near + jnp.dot(tally[s, rows, :], window[s * 256 : (s + 1) * 256, :], preferred_element_type=F32)
        total = []
        for u in range(STEP):
            lo = picked[pl.ds(u * 64, 32, stride=2), :].astype(BF16)
            hi = picked[pl.ds(u * 64 + 1, 32, stride=2), :].astype(BF16)
            o = jnp.broadcast_to(slot_cop[pl.ds(t0 + u, 1), :32], (NOPS, 32))
            hot = jnp.where(o == number, 1.0, 0.0).astype(BF16)
            far = jnp.dot(hot, jnp.concatenate([lo, hi], axis=1), preferred_element_type=F32)
            total.append(near[u * NOPS : (u + 1) * NOPS] + far)
        for r in range(0, NOPS, 8):
            parts = [transpose8([total[p * 8 + k][r : r + 8] for k in range(8)]) for p in range(STEP // 8)]
            for k in range(8):
                group[r + k, pl.ds(pl.multiple_of(t0, STEP), STEP), :] = jnp.concatenate(
                    [p[k] for p in parts], axis=0
                ).astype(BF16)

    gather(0, picked0)

    def two(i, _):
        t0 = i * (2 * STEP)
        gather(t0 + STEP, picked1)
        groups(t0, picked0)
        gather(jnp.minimum(t0 + 2 * STEP, TARGETS - STEP), picked0)
        groups(t0 + STEP, picked1)
        return 0

    lax.fori_loop(0, TARGETS // (2 * STEP), two, 0)

    weights.wait()
    out[...] = jnp.zeros_like(out)

    def translate(i, _):
        acc = out[...]
        for u in range(4):
            r = i * 4 + u
            acc = acc + lax.dot_general(group[r], ops[r], LAST, preferred_element_type=F32)
        out[...] = acc
        return 0

    lax.fori_loop(0, NOPS // 4, translate, 0)

    for stage in range(3):
        for h, k in hops:
            hop(h, stage, k).wait_send()
    for k in range(4):
        for h in range(2):
            to_sibling(h, k).wait_send()
    for k in range(2):
        halo(k).wait_send()


def local(
    multipole, coarse_multipole, operators, source_list, op_list, list_count, coarse_src, coarse_op
):
    here = pl.BlockSpec(memory_space=pl.ANY)
    vmem = pltpu.VMEM
    return pl.pallas_call(
        kernel,
        out_shape=jax.ShapeDtypeStruct((TARGETS, COEFFS), F32),
        in_specs=[here] * 8,
        out_specs=pl.BlockSpec(memory_space=vmem),
        scratch_shapes=[
            vmem((3 * 256, 256), BF16),
            vmem((4, 1024, 256), BF16),
            vmem((4096, 2, 128), F32),
            vmem((NOPS, 256, 256), BF16),
            vmem((SLOTS, 256), jnp.int32),
            vmem((SLOTS, 256), jnp.int32),
            vmem((1, 256), jnp.int32),
            vmem((COARSE_SLOTS, 256), jnp.int32),
            pltpu.SMEM((COARSE_SLOTS, 256), jnp.int32),
            vmem((256, 256), F32),
            vmem((256, 256), F32),
            vmem((256, 128), F32),
            vmem((256, 256), F32),
            vmem((3, TARGETS * NOPS, 256), BF16),
            vmem((STEP * 64, 128), F32),
            vmem((STEP * 64, 128), F32),
            vmem((NOPS, TARGETS, COEFFS), BF16),
            pltpu.SemaphoreType.DMA((9,)),
            pltpu.SemaphoreType.DMA((2, 3, 3)),
            pltpu.SemaphoreType.DMA((2, 3, 3)),
            pltpu.SemaphoreType.DMA((2, 4)),
            pltpu.SemaphoreType.DMA((2, 4)),
            pltpu.SemaphoreType.DMA((2,)),
            pltpu.SemaphoreType.DMA((2,)),
        ],
        compiler_params=pltpu.CompilerParams(
            collective_id=0, has_side_effects=True, vmem_limit_bytes=60 * 1024 * 1024
        ),
        cost_estimate=pl.CostEstimate(flops=14_000_000_000, bytes_accessed=12_000_000, transcendentals=0),
    )(
        multipole, coarse_multipole, operators, source_list.T, op_list.T, list_count.reshape(1, TARGETS),
        coarse_src.T, coarse_op.T,
    )


def solution(mesh):
    blocks = P(("gx", "gy"), None)
    placed = (blocks, blocks, P(), blocks, blocks, P(("gx", "gy")), blocks, blocks)
    return jax.shard_map(local, mesh=mesh, in_specs=placed, out_specs=blocks, check_vma=False)
```

time: 157 us -> 50.3 us (0.32)
  the two profiles are of different devices: /device:TPU:6 before, /device:TPU:1 now
where the time goes in v1:
time: 50.3 us; the launch traced here: 50.1 us
  Pallas kernels  48.4 us (96%)
  local copies, waits for them, and re-layouts  1.67 us (3%)
    pallas_call x1, Pallas kernels, local(): pl.pallas_call(kernel, out_shape=jax.ShapeDtypeStruct((TARGETS, COEFFS),...  48.4 us
    unnamed x1, local copies, waits for them, and re-layouts  1.67 us

profile of v1, /device:TPU:1, one launch (start us, length us, event | category | flops | bytes accessed | tf_op | source)
XLA Modules:
  0.0 50.1 jit_solution(17230497472233752176)
XLA Ops:
  0.0 48.4 %shard_map.82 = f32[256,256]{1,0:T(8,128)} custom-call(bf16[256,256]{1,0:T(8,128)(2,1)} %multipole.1, bf16[32,256]{1,0:T(8,128)(2,1)} %coarse.1, bf16[48,256,256]{2,1,0:T(8,128)(2,1)} %operators.1, s32[189,256]{1,0:T(8,128)} %bitcast.5, s32[189,256]{1,0:T(8,128)} %bitcast.6, s32[1,256]{1,0:T(1,128)} %bitcast.9, s32[27,256]{1,0:T(8,128)} %bitcast.7, ...), custom_call_target="tpu_custom_call" | custom-call | flops 14000000000 | bytes 12000000 | tf_op jit(solution)/shard_map/pallas_call | solution.py:272
  48.5 1.7 %copy.10 = f32[256,256]{1,0:T(8,128)} copy(f32[256,256]{1,0:T(8,128)} %shard_map.82) | data formatting | bytes 524288

commit v2 on v1

--- a/solution.py
+++ b/solution.py
@@ -13,6 +13,7 @@
 NOPS = 48
 COEFFS = 256
 STEP = 16
+RING = 4
 F8 = jnp.float8_e4m3fn
 BF16 = jnp.bfloat16
 F32 = jnp.float32
@@ -42,8 +43,8 @@
 def kernel(
     multipole, coarse, operators, source_t, op_t, count, coarse_src_t, coarse_op_t,
     out,
-    window, received, table, ops, src_v, op_v, count_v, cop_v, csrc, slot_q, slot_c, slot_cop, tmp, tally, picked0, picked1, group,
-    local_sem, send_sem, recv_sem, sib_send, sib_recv, halo_send, halo_recv,
+    window, received, table, ops, src_v, op_v, count_v, cop_v, csrc_v, index_v, index_s, slot_q, slot_c, slot_cop, cop_rows, tmp, tmp_i, tally, near, picked0, picked1, group,
+    local_sem, index_sem, send_sem, recv_sem, sib_send, sib_recv, halo_send, halo_recv,
 ):
     x = lax.axis_index("gx")
     gy = lax.axis_index("gy")
@@ -79,7 +80,7 @@
     mid = local(multipole, window.at[pl.ds(256, 256), :], 2)
     lists = [
         local(source_t, src_v, 3), local(op_t, op_v, 4), local(count, count_v, 5), local(coarse_op_t, cop_v, 6),
-        local(coarse_src_t, csrc, 7),
+        local(coarse_src_t, csrc_v, 7),
     ]
     weights = local(operators, ops, 8)
     for c in own + [mid] + lists + [weights]:
@@ -122,6 +123,14 @@
 
     hops = [(h, k) for k in (1, 3, 2) for h in range(2)]
 
+    for c in own + [mid]:
+        c.wait()
+    pl.semaphore_wait(barrier, len(partners))
+    for h, k in hops:
+        hop(h, 0, k).start()
+    halo(0).start()
+    halo(1).start()
+
     for c in lists[:3]:
         c.wait()
     place = src_v[...] - (me - 1) * TARGETS
@@ -133,31 +142,36 @@
     tmp[:SLOTS, :] = (place & 255).astype(F32)
     slot_c[...] = tmp[...].T
 
-    for c in own + [mid]:
-        c.wait()
-    pl.semaphore_wait(barrier, len(partners))
-    for h, k in hops:
-        hop(h, 0, k).start()
-    halo(0).start()
-    halo(1).start()
-
     for c in lists[3:]:
         c.wait()
     tmp[:128, :] = jnp.full((128, 256), -1.0, F32)
     tmp[:COARSE_SLOTS, :] = cop_v[...].astype(F32)
     slot_cop[...] = tmp[:128, :].T
+    for u in range(8):
+        cop_rows[:, u * 32 : (u + 1) * 32] = slot_cop[pl.ds(u, TARGETS // 8, stride=8), :][:, :32]
+    tmp_i[...] = jnp.zeros_like(tmp_i)
+    tmp_i[:COARSE_SLOTS, :] = csrc_v[...]
+    index_v[...] = tmp_i[...].T
     picked0[...] = jnp.zeros_like(picked0)
     picked1[...] = jnp.zeros_like(picked1)
 
+    def fetch(pair, k):
+        return pltpu.make_async_copy(
+            index_v.at[pl.ds(pl.multiple_of(pair * STEP, STEP), STEP), :], index_s.at[k], index_sem.at[k]
+        )
+
+    for k in range(RING):
+        fetch(k, k).start()
+
     def count_slots(i, _):
-        @pl.when(i == 3)
+        @pl.when(i == 6)
         def _():
             for h, k in hops:
                 hop(h, 0, k).wait_recv()
             for h, k in hops:
                 hop(h, 1, k).start()
 
-        @pl.when(i == 8)
+        @pl.when(i == 12)
         def _():
             for h, k in hops:
                 hop(h, 1, k).wait_recv()
@@ -179,80 +193,107 @@
 
     lax.fori_loop(0, TARGETS // STEP, count_slots, 0)
 
-    for k in (1, 3, 2):
-        for h in range(2):
-            hop(h, 2, k).wait_recv()
-            to_sibling(h, k).start()
     for k in range(2):
         halo(k).wait_recv()
+
+    def near_groups(i, _):
+        @pl.when(i == 10)
+        def _():
+            for k in (1, 3, 2):
+                for h in range(2):
+                    hop(h, 2, k).wait_recv()
+                    to_sibling(h, k).start()
+
+        t0 = i * STEP
+        rows = pl.ds(pl.multiple_of(t0 * NOPS, STEP * NOPS), STEP * NOPS)
+        acc = jnp.zeros((STEP * NOPS, COEFFS), F32)
+        for s in range(3):
+            acc = acc + jnp.dot(tally[s, rows, :], window[s * 256 : (s + 1) * 256, :], preferred_element_type=F32)
+        for r in range(0, NOPS, 8):
+            for p in range(STEP // 8):
+                first = [(p * 8 + k) * NOPS + r for k in range(8)]
+                turned = transpose8([acc[a : a + 8] for a in first])
+                for k in range(8):
+                    near[r + k, pl.ds(pl.multiple_of(t0 + 8 * p, 8), 8), :] = turned[k]
+        return 0
+
+    lax.fori_loop(0, TARGETS // STEP, near_groups, 0)
+
+    def fill(cc):
+        def chip(i, _):
+            at_chip = (lax.div(i, 16), lax.rem(lax.div(i, 4), 4), lax.rem(i, 4))
+            for h in range(2):
+                a, b, c = (
+                    at_chip[ORDERS[h][s]] * (1 - cc) + at_chip[ORDERS[2 + h][s]] * cc for s in range(3)
+                )
+                v = received[cc * 2 + h, pl.ds(pl.multiple_of((c * 16 + b * 4 + a) * 16, 16), 16), :].astype(F32)
+                row = pl.ds(pl.multiple_of(i * 64 + cc * 32 + h * 16, 16), 16)
+                table[row, 0, :] = v[:, :128]
+                table[row, 1, :] = v[:, 128:]
+            return 0
+
+        lax.fori_loop(0, 64, chip, 0)
+
+    fill(core)
     for k in (0, 1, 3, 2):
         for h in range(2):
             to_sibling(h, k).wait_recv()
-
-    def fill(i, _):
-        cx, cy, cz = lax.div(i, 16), lax.rem(lax.div(i, 4), 4), lax.rem(i, 4)
-        chip = (cx, cy, cz)
-        for f in range(4):
-            a, b, c = (chip[ORDERS[f][s]] for s in range(3))
-            v = received[f, pl.ds(pl.multiple_of((c * 16 + b * 4 + a) * 16, 16), 16), :].astype(F32)
-            row = pl.ds(pl.multiple_of(i * 64 + f * 16, 16), 16)
-            table[row, 0, :] = v[:, :128]
-            table[row, 1, :] = v[:, 128:]
-        return 0
-
-    lax.fori_loop(0, 64, fill, 0)
-
-    number = lax.broadcasted_iota(jnp.int32, (NOPS, 32), 0).astype(F32)
-
-    def gather(t0, picked):
+    fill(1 - core)
+
+    row_no = lax.broadcasted_iota(jnp.int32, (16, 256), 0)
+    same = (row_no & 7) == lax.shift_right_logical(lax.broadcasted_iota(jnp.int32, (16, 256), 1), 5)
+    number = lax.shift_right_logical(row_no, 3).astype(F32)
+
+    def gather(k, picked):
         for u in range(STEP):
             for j in range(COARSE_SLOTS):
-                picked[pl.ds((u * 32 + j) * 2, 2), :] = table[csrc[j, t0 + u]]
-
-    def groups(t0, picked):
-        rows = pl.ds(pl.multiple_of(t0 * NOPS, STEP * NOPS), STEP * NOPS)
-        near = jnp.zeros((STEP * NOPS, COEFFS), F32)
-        for s in range(3):
-            near = near + jnp.dot(tally[s, rows, :], window[s * 256 : (s + 1) * 256, :], preferred_element_type=F32)
-        total = []
-        for u in range(STEP):
-            lo = picked[pl.ds(u * 64, 32, stride=2), :].astype(BF16)
-            hi = picked[pl.ds(u * 64 + 1, 32, stride=2), :].astype(BF16)
-            o = jnp.broadcast_to(slot_cop[pl.ds(t0 + u, 1), :32], (NOPS, 32))
-            hot = jnp.where(o == number, 1.0, 0.0).astype(BF16)
-            far = jnp.dot(hot, jnp.concatenate([lo, hi], axis=1), preferred_element_type=F32)
-            total.append(near[u * NOPS : (u + 1) * NOPS] + far)
-        for r in range(0, NOPS, 8):
-            parts = [transpose8([total[p * 8 + k][r : r + 8] for k in range(8)]) for p in range(STEP // 8)]
-            for k in range(8):
-                group[r + k, pl.ds(pl.multiple_of(t0, STEP), STEP), :] = jnp.concatenate(
-                    [p[k] for p in parts], axis=0
-                ).astype(BF16)
-
+                picked[pl.ds((u * 32 + j) * 2, 2), :] = table[index_s[k, u, j]]
+
+    def far(eight, picked, p):
+        lo = picked[pl.ds(512 * p, 256, stride=2), :].astype(BF16)
+        hi = picked[pl.ds(512 * p + 1, 256, stride=2), :].astype(BF16)
+        o = jnp.broadcast_to(cop_rows[pl.ds(eight, 1), :], (16, 256))
+        o = jnp.where(same, o, -1.0).astype(BF16)
+        hot = jnp.concatenate(
+            [jnp.where(o == (number + 2.0 * k).astype(BF16), BF16(1), BF16(0)) for k in range(NOPS // 2)], axis=0
+        )
+        return jnp.dot(hot, jnp.concatenate([lo, hi], axis=1), preferred_element_type=F32)
+
+    picked = (picked0, picked1)
+    pairs = TARGETS // STEP
+    fetch(0, 0).wait()
     gather(0, picked0)
-
-    def two(i, _):
-        t0 = i * (2 * STEP)
-        gather(t0 + STEP, picked1)
-        groups(t0, picked0)
-        gather(jnp.minimum(t0 + 2 * STEP, TARGETS - STEP), picked0)
-        groups(t0 + STEP, picked1)
+    fetch(RING, 0).start()
+
+    def coarse_groups(i, _):
+        for k in range(RING):
+            pair, nxt = i * RING + k, (k + 1) % RING
+            fetch(0, nxt).wait()
+            gather(nxt, picked[(k + 1) % 2])
+            fetch(jnp.minimum(pair + 1 + RING, pairs - 1), nxt).start()
+            f0, f1 = far(2 * pair, picked[k % 2], 0), far(2 * pair + 1, picked[k % 2], 1)
+            at_t = pl.ds(pl.multiple_of(pair * STEP, STEP), STEP)
+            for r in range(NOPS):
+                both = jnp.concatenate([f0[r * 8 : r * 8 + 8], f1[r * 8 : r * 8 + 8]], axis=0)
+                group[r, at_t, :] = (near[r, at_t, :] + both).astype(BF16)
         return 0
 
-    lax.fori_loop(0, TARGETS // (2 * STEP), two, 0)
+    lax.fori_loop(0, pairs // RING, coarse_groups, 0)
+    for k in range(RING):
+        fetch(0, k).wait()
 
     weights.wait()
     out[...] = jnp.zeros_like(out)
 
     def translate(i, _):
         acc = out[...]
-        for u in range(4):
-            r = i * 4 + u
+        for u in range(16):
+            r = i * 16 + u
             acc = acc + lax.dot_general(group[r], ops[r], LAST, preferred_element_type=F32)
         out[...] = acc
         return 0
 
-    lax.fori_loop(0, NOPS // 4, translate, 0)
+    lax.fori_loop(0, NOPS // 16, translate, 0)
 
     for stage in range(3):
         for h, k in hops:
@@ -271,7 +312,7 @@
     vmem = pltpu.VMEM
     return pl.pallas_call(
         kernel,
-        out_shape=jax.ShapeDtypeStruct((TARGETS, COEFFS), F32),
+        out_shape=vmem((TARGETS, COEFFS), F32),
         in_specs=[here] * 8,
         out_specs=pl.BlockSpec(memory_space=vmem),
         scratch_shapes=[
@@ -283,16 +324,22 @@
             vmem((SLOTS, 256), jnp.int32),
             vmem((1, 256), jnp.int32),
             vmem((COARSE_SLOTS, 256), jnp.int32),
-            pltpu.SMEM((COARSE_SLOTS, 256), jnp.int32),
+            vmem((COARSE_SLOTS, 256), jnp.int32),
+            vmem((256, 128), jnp.int32),
+            pltpu.SMEM((RING, STEP, 128), jnp.int32),
             vmem((256, 256), F32),
             vmem((256, 256), F32),
             vmem((256, 128), F32),
+            vmem((TARGETS // 8, 256), F32),
             vmem((256, 256), F32),
+            vmem((128, 256), jnp.int32),
             vmem((3, TARGETS * NOPS, 256), BF16),
+            vmem((NOPS, TARGETS, COEFFS), F32),
             vmem((STEP * 64, 128), F32),
             vmem((STEP * 64, 128), F32),
             vmem((NOPS, TARGETS, COEFFS), BF16),
             pltpu.SemaphoreType.DMA((9,)),
+            pltpu.SemaphoreType.DMA((RING,)),
             pltpu.SemaphoreType.DMA((2, 3, 3)),
             pltpu.SemaphoreType.DMA((2, 3, 3)),
             pltpu.SemaphoreType.DMA((2, 4)),

time: 50.3 us -> 45.1 us (0.90)
  the two profiles are of different devices: /device:TPU:1 before, /device:TPU:0 now
where the time goes in v2:
time: 45.1 us; the launch traced here: 45 us
  Pallas kernels  44.3 us (98%)
  local copies, waits for them, and re-layouts  0.71 us (2%)
    pallas_call x1, Pallas kernels, local(): pl.pallas_call(kernel, out_shape=vmem((TARGETS, COEFFS), F32), in_specs=[...  44.3 us

profile of v2, /device:TPU:0, one launch (start us, length us, event | category | flops | bytes accessed | tf_op | source)
XLA Modules:
  0.0 45.0 jit_solution(10649218919390010402)
XLA Ops:
  0.0 44.3 %shard_map.82 = f32[256,256]{1,0:T(8,128)S(1)} custom-call(bf16[256,256]{1,0:T(8,128)(2,1)} %multipole.1, bf16[32,256]{1,0:T(8,128)(2,1)} %coarse.1, bf16[48,256,256]{2,1,0:T(8,128)(2,1)} %operators.1, s32[189,256]{1,0:T(8,128)} %bitcast.5, s32[189,256]{1,0:T(8,128)} %bitcast.6, s32[1,256]{1,0:T(1,128)} %bitcast.9, s32[27,256]{1,0:T(8,128)} %bitcast.7, ...), custom_call_target="tpu_custom_call" | custom-call | flops 14000000000 | bytes 12000000 | tf_op jit(solution)/shard_map/pallas_call | solution.py:313
  44.3 0.7 %copy.10 = f32[256,256]{1,0:T(8,128)} copy(f32[256,256]{1,0:T(8,128)S(1)} %shard_map.82) | data formatting | bytes 524288

commit v3 on v2

--- a/solution.py
+++ b/solution.py
@@ -123,14 +123,6 @@
 
     hops = [(h, k) for k in (1, 3, 2) for h in range(2)]
 
-    for c in own + [mid]:
-        c.wait()
-    pl.semaphore_wait(barrier, len(partners))
-    for h, k in hops:
-        hop(h, 0, k).start()
-    halo(0).start()
-    halo(1).start()
-
     for c in lists[:3]:
         c.wait()
     place = src_v[...] - (me - 1) * TARGETS
@@ -164,14 +156,24 @@
         fetch(k, k).start()
 
     def count_slots(i, _):
-        @pl.when(i == 6)
+        @pl.when(i == 4)
         def _():
+            for c in own + [mid]:
+                c.wait()
+            pl.semaphore_wait(barrier, len(partners))
+            for h, k in hops:
+                hop(h, 0, k).start()
+            halo(0).start()
+            halo(1).start()
+
+        @pl.when(i == 10)
+        def _():
             for h, k in hops:
                 hop(h, 0, k).wait_recv()
             for h, k in hops:
                 hop(h, 1, k).start()
 
-        @pl.when(i == 12)
+        @pl.when(i == 15)
         def _():
             for h, k in hops:
                 hop(h, 1, k).wait_recv()
@@ -197,7 +199,7 @@
         halo(k).wait_recv()
 
     def near_groups(i, _):
-        @pl.when(i == 10)
+        @pl.when(i == 13)
         def _():
             for k in (1, 3, 2):
                 for h in range(2):
@@ -219,26 +221,30 @@
 
     lax.fori_loop(0, TARGETS // STEP, near_groups, 0)
 
-    def fill(cc):
+    def fill(cc, last):
+        scale = [
+            [4 ** (2 - ORDERS[h][s]) * (1 - cc) + 4 ** (2 - ORDERS[2 + h][s]) * cc for s in range(3)] for h in range(2)
+        ]
+
         def chip(i, _):
-            at_chip = (lax.div(i, 16), lax.rem(lax.div(i, 4), 4), lax.rem(i, 4))
+            b, a = lax.div(i, 4), lax.rem(i, 4)
             for h in range(2):
-                a, b, c = (
-                    at_chip[ORDERS[h][s]] * (1 - cc) + at_chip[ORDERS[2 + h][s]] * cc for s in range(3)
-                )
-                v = received[cc * 2 + h, pl.ds(pl.multiple_of((c * 16 + b * 4 + a) * 16, 16), 16), :].astype(F32)
-                row = pl.ds(pl.multiple_of(i * 64 + cc * 32 + h * 16, 16), 16)
+                v = received[cc * 2 + h, pl.ds(pl.multiple_of((last[h] * 16 + i) * 16, 16), 16), :].astype(F32)
+                place = a * scale[h][0] + b * scale[h][1] + last[h] * scale[h][2]
+                row = pl.ds(pl.multiple_of(place * 64 + cc * 32 + h * 16, 16), 16)
                 table[row, 0, :] = v[:, :128]
                 table[row, 1, :] = v[:, 128:]
             return 0
 
-        lax.fori_loop(0, 64, chip, 0)
-
-    fill(core)
+        lax.fori_loop(0, 16, chip, 0)
+
+    for k in range(4):
+        fill(core, [lax.rem(at[h][2] + 4 - k, 4) for h in range(2)])
+    beside = [coords[ORDERS[h][2]] * core + coords[ORDERS[2 + h][2]] * (1 - core) for h in range(2)]
     for k in (0, 1, 3, 2):
         for h in range(2):
             to_sibling(h, k).wait_recv()
-    fill(1 - core)
+        fill(1 - core, [lax.rem(beside[h] + 4 - k, 4) for h in range(2)])
 
     row_no = lax.broadcasted_iota(jnp.int32, (16, 256), 0)
     same = (row_no & 7) == lax.shift_right_logical(lax.broadcasted_iota(jnp.int32, (16, 256), 1), 5)

time: 45.1 us -> 43.3 us (0.960)
  Pallas kernels: 44.3 us -> 42.5 us
    pallas_call x1, Pallas kernels: 44.3 us -> 42.5 us  [local(): pl.pallas_call(kernel, out_shape=vmem((TARGETS, COEFFS), F32), in_specs=[...]
where the time goes in v3:
time: 43.3 us; the launch traced here: 43.2 us
  Pallas kernels  42.5 us (98%)
  local copies, waits for them, and re-layouts  0.71 us (2%)
    pallas_call x1, Pallas kernels, local(): pl.pallas_call(kernel, out_shape=vmem((TARGETS, COEFFS), F32), in_specs=[...  42.5 us

profile of v3, /device:TPU:0, one launch (start us, length us, event | category | flops | bytes accessed | tf_op | source)
XLA Modules:
  0.0 43.2 jit_solution(13366139528074585693)
XLA Ops:
  0.0 42.5 %shard_map.82 = f32[256,256]{1,0:T(8,128)S(1)} custom-call(bf16[256,256]{1,0:T(8,128)(2,1)} %multipole.1, bf16[32,256]{1,0:T(8,128)(2,1)} %coarse.1, bf16[48,256,256]{2,1,0:T(8,128)(2,1)} %operators.1, s32[189,256]{1,0:T(8,128)} %bitcast.5, s32[189,256]{1,0:T(8,128)} %bitcast.6, s32[1,256]{1,0:T(1,128)} %bitcast.9, s32[27,256]{1,0:T(8,128)} %bitcast.7, ...), custom_call_target="tpu_custom_call" | custom-call | flops 14000000000 | bytes 12000000 | tf_op jit(solution)/shard_map/pallas_call | solution.py:319
  42.5 0.7 %copy.10 = f32[256,256]{1,0:T(8,128)} copy(f32[256,256]{1,0:T(8,128)S(1)} %shard_map.82) | data formatting | bytes 524288
